TPU v7x, 32 devices: a whole 2x2x4 slice. The times are simulated.
32 devices in a mesh: dp: 2 (over y), fsdp: 16 (over z, x, core).
Axes of the slice: x: 2, y: 2, z: 4, core: 2. Of those that a mesh axis runs over, the one named last changes fastest.
Arguments:
- content_in: bfloat16 [96, 512, 768], P(('dp', 'fsdp')), may hold values from -6 to 6
- query_in: bfloat16 [96, 77, 768], P(('dp', 'fsdp')), may hold values from -6 to 6
- permutation: int32 [96, 512], P(('dp', 'fsdp')), may hold values from 0 to 511, each once within a row
- query_weight: bfloat16 [768, 768], P('fsdp'), may hold values from -0.21875 to 0.21875
- key_weight: bfloat16 [768, 768], P('fsdp'), may hold values from -0.21875 to 0.21875
- value_weight: bfloat16 [768, 768], P('fsdp'), may hold values from -0.21875 to 0.21875
- output_weight: bfloat16 [768, 768], P('fsdp'), may hold values from -2 to 2
- inner_weight: bfloat16 [768, 3072], P('fsdp'), may hold values from -0.21875 to 0.21875
- outer_weight: bfloat16 [3072, 768], P('fsdp'), may hold values from -0.109375 to 0.109375
- query_bias: bfloat16 [768], P('fsdp'), may hold values from -3 to 3
- value_bias: bfloat16 [768], P('fsdp'), may hold values from -3 to 3
- output_bias: bfloat16 [768], P('fsdp'), may hold values from -3 to 3
- first_gain: bfloat16 [768], P('fsdp'), may hold values from 0.099609375 to 1.8984375
- first_shift: bfloat16 [768], P('fsdp'), may hold values from -3 to 3
- inner_bias: bfloat16 [3072], P('fsdp'), may hold values from -3 to 3
- outer_bias: bfloat16 [768], P('fsdp'), may hold values from -3 to 3
- second_gain: bfloat16 [768], P('fsdp'), may hold values from 0.099609375 to 1.8984375
- second_shift: bfloat16 [768], P('fsdp'), may hold values from -3 to 3
- bias_table: bfloat16 [384], P('fsdp'), may hold values from -4 to 4
- content_cotangent: bfloat16 [96, 512, 768], P(('dp', 'fsdp')), may hold values from -6 to 6
- query_cotangent: bfloat16 [96, 77, 768], P(('dp', 'fsdp')), may hold values from -6 to 6
Outputs:
- content_out: bfloat16 [96, 512, 768], P(('dp', 'fsdp'))
- query_out: bfloat16 [96, 77, 768], P(('dp', 'fsdp'))
- content_grad: float32 [96, 512, 768], P(('dp', 'fsdp'))
- query_grad: float32 [96, 77, 768], P(('dp', 'fsdp'))
- query_weight_grad: float32 [768, 768], P('fsdp')
- key_weight_grad: float32 [768, 768], P('fsdp')
- value_weight_grad: float32 [768, 768], P('fsdp')
- output_weight_grad: float32 [768, 768], P('fsdp')
- inner_weight_grad: float32 [768, 3072], P('fsdp')
- outer_weight_grad: float32 [3072, 768], P('fsdp')
- query_bias_grad: float32 [768], P('fsdp')
- value_bias_grad: float32 [768], P('fsdp')
- output_bias_grad: float32 [768], P('fsdp')
- first_gain_grad: float32 [768], P('fsdp')
- first_shift_grad: float32 [768], P('fsdp')
- inner_bias_grad: float32 [3072], P('fsdp')
- outer_bias_grad: float32 [768], P('fsdp')
- second_gain_grad: float32 [768], P('fsdp')
- second_shift_grad: float32 [768], P('fsdp')
- bias_table_grad: float32 [384], P('fsdp')
All inputs are finite; a program needn't handle non-finite values.
Results may differ from a plain program's by a relative error of at most 0.015.
Values may be sent and summed in bfloat16 or wider, within the bound.
A program may use at most 256 MiB of HBM per device.

v0:
```python
import jax
import jax.numpy as jnp
from jax import lax
from jax.sharding import PartitionSpec as P

D = 768
HEADS = 12
HEAD = 64
BUCKETS = 32
LEN = 512
PRED = 77


eps_norm = 1e-05
inverse_root = 0.7071067811865476
density_scale = 0.3989422804014327
bucket_edges = (12, 16, 23, 32, 46, 64, 91)


def shortened(value):
    return jax.tree.map(lambda a: a.astype(jnp.bfloat16) if a.dtype == jnp.float32 else a, value)


def bucket_index(relative):
    distance = jnp.abs(relative)
    coarse = 8 + sum(((distance >= boundary).astype(jnp.int32) for boundary in bucket_edges))
    within = jnp.where(distance < 8, distance, coarse)
    return within + 16 * (relative > 0).astype(jnp.int32)


def layout(order_row):
    length = order_row.shape[0]
    ranking = jnp.zeros((length,), jnp.int32).at[order_row].set(jnp.arange(length, dtype=jnp.int32))
    positions = jnp.concatenate([jnp.arange(length, dtype=jnp.int32), order_row[length - PRED :]])
    limits = jnp.concatenate(
        [
            jnp.maximum(ranking, length - PRED - 1),
            jnp.arange(PRED, dtype=jnp.int32) + (length - PRED - 1),
        ]
    )
    visible = ranking[None, :] <= limits[:, None]
    buckets = bucket_index(jnp.arange(length, dtype=jnp.int32)[None, :] - positions[:, None])
    onehot = (buckets[:, :, None] == jnp.arange(BUCKETS, dtype=jnp.int32)).astype(jnp.bfloat16)
    return (visible, onehot)


def norm_rows(values, gain_row, shift_row):
    centered = values - jnp.mean(values, axis=-1, keepdims=True)
    variance = jnp.mean(centered * centered, axis=-1, keepdims=True)
    return centered * lax.rsqrt(variance + eps_norm) * gain_row + shift_row


def gelu_slope(values):
    return (
        0.5 * (1.0 + lax.erf(values * inverse_root))
        + values * jnp.exp(-0.5 * values * values) * density_scale
    )


def project(left, right_matrix):
    return jnp.einsum("srd,de->sre", left, right_matrix, preferred_element_type=jnp.float32)


def project_back(left, right_matrix):
    return jnp.einsum("sre,de->srd", left, right_matrix, preferred_element_type=jnp.float32)


def outer_sum(left, right_rows):
    return jnp.einsum("srd,sre->de", left, right_rows, preferred_element_type=jnp.float32)


def row_sum(values):
    return jnp.sum(values, axis=(0, 1), dtype=jnp.float32)


def per_device(
    content_in,
    query_in,
    permutation,
    query_weight,
    key_weight,
    value_weight,
    output_weight,
    inner_weight,
    outer_weight,
    query_bias,
    value_bias,
    output_bias,
    first_gain,
    first_shift,
    inner_bias,
    outer_bias,
    second_gain,
    second_shift,
    bias_table,
    content_cotangent,
    query_cotangent,
):
    (
        query_full,
        key_full,
        value_full,
        output_full,
        inner_full,
        outer_full,
        bias_query,
        bias_value,
        bias_output,
        gain_first,
        shift_first,
        bias_inner,
        bias_outer,
        gain_second,
        shift_second,
        table_flat,
    ) = (
        lax.all_gather(query_weight, "fsdp", axis=0, tiled=True),
        lax.all_gather(key_weight, "fsdp", axis=0, tiled=True),
        lax.all_gather(value_weight, "fsdp", axis=0, tiled=True),
        lax.all_gather(output_weight, "fsdp", axis=0, tiled=True),
        lax.all_gather(inner_weight, "fsdp", axis=0, tiled=True),
        lax.all_gather(outer_weight, "fsdp", axis=0, tiled=True),
        lax.all_gather(query_bias, "fsdp", axis=0, tiled=True),
        lax.all_gather(value_bias, "fsdp", axis=0, tiled=True),
        lax.all_gather(output_bias, "fsdp", axis=0, tiled=True),
        lax.all_gather(first_gain, "fsdp", axis=0, tiled=True),
        lax.all_gather(first_shift, "fsdp", axis=0, tiled=True),
        lax.all_gather(inner_bias, "fsdp", axis=0, tiled=True),
        lax.all_gather(outer_bias, "fsdp", axis=0, tiled=True),
        lax.all_gather(second_gain, "fsdp", axis=0, tiled=True),
        lax.all_gather(second_shift, "fsdp", axis=0, tiled=True),
        lax.all_gather(bias_table, "fsdp", axis=0, tiled=True),
    )
    score_scale = HEAD ** (-0.5)
    bucket_table = table_flat.reshape(BUCKETS, HEADS)
    stacked = jnp.concatenate([content_in, query_in], axis=1)
    row_count = stacked.shape[1]
    queries = (project(stacked, query_full) + bias_query).astype(jnp.bfloat16)
    keys_all = project(content_in, key_full).astype(jnp.bfloat16)
    values_all = (project(content_in, value_full) + bias_value).astype(jnp.bfloat16)

    def scores_of(query_rows, key_rows, onehot, visible):
        products = jnp.einsum(
            "qhe,khe->hqk",
            query_rows.reshape(row_count, HEADS, HEAD),
            key_rows.reshape(LEN, HEADS, HEAD),
            preferred_element_type=jnp.float32,
        )
        biases = jnp.einsum("qkb,bh->hqk", onehot, bucket_table, preferred_element_type=jnp.float32)
        return jnp.where(visible[None], products * score_scale + biases, -1000000000.0)

    def attend(inputs):
        query_rows, key_rows, value_rows, order_row = inputs
        visible, onehot = layout(order_row)
        scores = scores_of(query_rows, key_rows, onehot, visible)
        row_peak = jnp.max(scores, axis=-1, keepdims=True)
        exponent = jnp.exp(scores - row_peak)
        row_total = jnp.sum(exponent, axis=-1, keepdims=True)
        attention = (exponent / row_total).astype(jnp.bfloat16)
        mixture = jnp.einsum(
            "hqk,khe->qhe",
            attention,
            value_rows.reshape(LEN, HEADS, HEAD),
            preferred_element_type=jnp.float32,
        )
        return (
            mixture.reshape(row_count, D).astype(jnp.bfloat16),
            (row_peak + jnp.log(row_total))[..., 0],
        )

    mixture, logsum = lax.map(attend, (queries, keys_all, values_all, permutation))
    gain_one = gain_first.astype(jnp.float32)
    shift_one = shift_first.astype(jnp.float32)
    gain_two = gain_second.astype(jnp.float32)
    shift_two = shift_second.astype(jnp.float32)
    first_in = stacked.astype(jnp.float32) + project(mixture, output_full) + bias_output
    normed_one = norm_rows(first_in, gain_one, shift_one)
    first_low = normed_one.astype(jnp.bfloat16)
    hidden_pre = project(first_low, inner_full) + bias_inner
    activated = (0.5 * hidden_pre * (1.0 + lax.erf(hidden_pre * inverse_root))).astype(jnp.bfloat16)
    second_in = normed_one + project(activated, outer_full) + bias_outer
    result = norm_rows(second_in, gain_two, shift_two)
    content_out = result[:, :LEN].astype(jnp.bfloat16)
    query_out = result[:, LEN:].astype(jnp.bfloat16)
    (
        back_query,
        back_key,
        back_value,
        back_output,
        back_inner,
        back_outer,
        back_gain_one,
        back_gain_two,
    ) = (
        lax.all_gather(query_weight, "fsdp", axis=0, tiled=True),
        lax.all_gather(key_weight, "fsdp", axis=0, tiled=True),
        lax.all_gather(value_weight, "fsdp", axis=0, tiled=True),
        lax.all_gather(output_weight, "fsdp", axis=0, tiled=True),
        lax.all_gather(inner_weight, "fsdp", axis=0, tiled=True),
        lax.all_gather(outer_weight, "fsdp", axis=0, tiled=True),
        lax.all_gather(first_gain, "fsdp", axis=0, tiled=True),
        lax.all_gather(second_gain, "fsdp", axis=0, tiled=True),
    )
    cotangent = jnp.concatenate([content_cotangent, query_cotangent], axis=1).astype(jnp.float32)
    unused_two, norm_back_two = jax.vjp(
        norm_rows, second_in, back_gain_two.astype(jnp.float32), shift_two
    )
    second_back, gain_two_grad, shift_two_grad = norm_back_two(cotangent)
    outer_delta = second_back.astype(jnp.bfloat16)
    outer_bias_grad = row_sum(outer_delta)
    outer_weight_grad = outer_sum(activated, outer_delta)
    inner_delta = (project_back(outer_delta, back_outer) * gelu_slope(hidden_pre)).astype(
        jnp.bfloat16
    )
    inner_bias_grad = row_sum(inner_delta)
    inner_weight_grad = outer_sum(first_low, inner_delta)
    first_back = second_back + project_back(inner_delta, back_inner)
    unused_one, norm_back_one = jax.vjp(
        norm_rows, first_in, back_gain_one.astype(jnp.float32), shift_one
    )
    first_in_back, gain_one_grad, shift_one_grad = norm_back_one(first_back)
    output_delta = first_in_back.astype(jnp.bfloat16)
    output_bias_grad = row_sum(output_delta)
    output_weight_grad = outer_sum(mixture, output_delta)
    mixture_delta = project_back(output_delta, back_output).astype(jnp.bfloat16)

    def attend_back(inputs):
        query_rows, key_rows, value_rows, order_row, lse_row, delta_rows = inputs
        visible, onehot = layout(order_row)
        scores = scores_of(query_rows, key_rows, onehot, visible)
        attention = jnp.exp(scores - lse_row[:, :, None])
        attention_low = attention.astype(jnp.bfloat16)
        delta_heads = delta_rows.reshape(row_count, HEADS, HEAD)
        value_heads = value_rows.reshape(LEN, HEADS, HEAD)
        key_heads = key_rows.reshape(LEN, HEADS, HEAD)
        query_heads = query_rows.reshape(row_count, HEADS, HEAD)
        value_delta = jnp.einsum(
            "hqk,qhe->khe", attention_low, delta_heads, preferred_element_type=jnp.float32
        )
        weight_delta = jnp.einsum(
            "qhe,khe->hqk", delta_heads, value_heads, preferred_element_type=jnp.float32
        )
        score_delta = attention * (
            weight_delta - jnp.sum(weight_delta * attention, axis=-1, keepdims=True)
        )
        score_delta = score_delta.astype(jnp.bfloat16)
        table_delta = jnp.einsum(
            "hqk,qkb->bh", score_delta, onehot, preferred_element_type=jnp.float32
        )
        query_delta = (
            jnp.einsum("hqk,khe->qhe", score_delta, key_heads, preferred_element_type=jnp.float32)
            * score_scale
        )
        key_delta = (
            jnp.einsum("hqk,qhe->khe", score_delta, query_heads, preferred_element_type=jnp.float32)
            * score_scale
        )
        return (
            query_delta.reshape(row_count, D).astype(jnp.bfloat16),
            key_delta.reshape(LEN, D).astype(jnp.bfloat16),
            value_delta.reshape(LEN, D).astype(jnp.bfloat16),
            table_delta,
        )

    query_delta, key_delta, value_delta, table_delta = lax.map(
        attend_back, (queries, keys_all, values_all, permutation, logsum, mixture_delta)
    )
    table_grad = jnp.sum(table_delta, axis=0).reshape(BUCKETS * HEADS)
    query_weight_grad = outer_sum(stacked, query_delta)
    query_bias_grad = row_sum(query_delta)
    key_weight_grad = outer_sum(content_in, key_delta)
    value_weight_grad = outer_sum(content_in, value_delta)
    value_bias_grad = row_sum(value_delta)
    stacked_back = first_in_back + project_back(query_delta, back_query)
    content_grad = (
        stacked_back[:, :LEN]
        + project_back(key_delta, back_key)
        + project_back(value_delta, back_value)
    )
    query_grad = stacked_back[:, LEN:]
    shares = (
        lax.psum_scatter(query_weight_grad, "fsdp", scatter_dimension=0, tiled=True),
        lax.psum_scatter(key_weight_grad, "fsdp", scatter_dimension=0, tiled=True),
        lax.psum_scatter(value_weight_grad, "fsdp", scatter_dimension=0, tiled=True),
        lax.psum_scatter(output_weight_grad, "fsdp", scatter_dimension=0, tiled=True),
        lax.psum_scatter(inner_weight_grad, "fsdp", scatter_dimension=0, tiled=True),
        lax.psum_scatter(outer_weight_grad, "fsdp", scatter_dimension=0, tiled=True),
        lax.psum_scatter(query_bias_grad, "fsdp", scatter_dimension=0, tiled=True),
        lax.psum_scatter(value_bias_grad, "fsdp", scatter_dimension=0, tiled=True),
        lax.psum_scatter(output_bias_grad, "fsdp", scatter_dimension=0, tiled=True),
        lax.psum_scatter(gain_one_grad, "fsdp", scatter_dimension=0, tiled=True),
        lax.psum_scatter(shift_one_grad, "fsdp", scatter_dimension=0, tiled=True),
        lax.psum_scatter(inner_bias_grad, "fsdp", scatter_dimension=0, tiled=True),
        lax.psum_scatter(outer_bias_grad, "fsdp", scatter_dimension=0, tiled=True),
        lax.psum_scatter(gain_two_grad, "fsdp", scatter_dimension=0, tiled=True),
        lax.psum_scatter(shift_two_grad, "fsdp", scatter_dimension=0, tiled=True),
        lax.psum_scatter(table_grad, "fsdp", scatter_dimension=0, tiled=True),
    )
    totals = jax.tree.map(
        lambda part: part.astype(jnp.float32), lax.psum(shortened(tuple(shares)), "dp")
    )
    return (content_out, query_out, content_grad, query_grad) + tuple(totals)


def solution(mesh):
    placed = (
        P(("dp", "fsdp"), None, None),
        P(("dp", "fsdp"), None, None),
        P(("dp", "fsdp"), None),
        P("fsdp", None),
        P("fsdp", None),
        P("fsdp", None),
        P("fsdp", None),
        P("fsdp", None),
        P("fsdp", None),
        P("fsdp"),
        P("fsdp"),
        P("fsdp"),
        P("fsdp"),
        P("fsdp"),
        P("fsdp"),
        P("fsdp"),
        P("fsdp"),
        P("fsdp"),
        P("fsdp"),
        P(("dp", "fsdp"), None, None),
        P(("dp", "fsdp"), None, None),
    )
    return jax.shard_map(
        per_device,
        mesh=mesh,
        in_specs=placed,
        out_specs=(
            P(("dp", "fsdp"), None, None),
            P(("dp", "fsdp"), None, None),
            P(("dp", "fsdp"), None, None),
            P(("dp", "fsdp"), None, None),
            P("fsdp", None),
            P("fsdp", None),
            P("fsdp", None),
            P("fsdp", None),
            P("fsdp", None),
            P("fsdp", None),
            P("fsdp"),
            P("fsdp"),
            P("fsdp"),
            P("fsdp"),
            P("fsdp"),
            P("fsdp"),
            P("fsdp"),
            P("fsdp"),
            P("fsdp"),
            P("fsdp"),
        ),
        check_vma=False,
    )
```

profile of v0, /device:TPU:0, one launch (start us, length us, event | category | flops | bytes accessed | tf_op | source)
XLA Modules:
  0.0 1198.7 jit_solution(13830392546817639019)
XLA Ops:
  23.0 63.2 %all-reduce.21 = (bf16[768]{0:T(1024)(128)(2,1)S(1)}, bf16[384]{0:T(512)(128)(2,1)S(1)}, bf16[768]{0:T(1024)(128)(2,1)S(1)}, bf16[768]{0:T(1024)(128)(2,1)S(1)},...) all-reduce(bf16[768]{0:T(1024)(128)(2,1)S(1)} %dynamic-update-slice, ...), channel_id=1, replica_groups=mesh['dp'=2,'fsdp'=16] {'fsdp'}, use_global_device_ids=true, to_apply=%add.1 | all-reduce | flops 9600 | bytes 38400
  112.5 18.5 %all-gather.9.cloned.1.call-done = bf16[768,768]{1,0:T(8,128)(2,1)} async-done(((bf16[48,768]{1,0:T(8,128)(2,1)}), bf16[768,768]{1,0:T(8,128)(2,1)}) %all-gather.9.cloned.1.call-update) | async-done | bytes 1179664 | tf_op jit(solution)/shard_map/all_gather | solution.py:117
  139.0 156.7 %while.28 = (s32[]{:T(128)}, bf16[3,589,768]{1,2,0:T(8,128)(2,1)S(1)}, f32[3,12,589]{2,1,0:T(8,128)S(1)}, bf16[3,512,768]{1,2,0:T(8,128)(2,1)}, s32[3,512]{1,0:T...) while((s32[]{:T(128)}, ...), condition=%wide.region_4.5_spmd, body=%wide.region_0.4_spmd.sunk | while | flops 1209434752 | bytes 143893200 | solution.py:171
  146.0 9.7 fusion.162
  155.8 20.9 %fusion.163 = (f32[12,589]{1,0:T(8,128)S(1)}, f32[12,589,512]{2,1,0:T(8,128)}) fusion(f32[589,512,12]{1,2,0:T(8,128)} %fusion.162, bf16[589,12,64]{0,2,1:T(8,128)(2,1)S(1)} %bitcast.237, bf16[512,12,64]{0,2,1:T(8,128)(2,1)S(1)} %bitcast.241, pred[589,512]{1,0:T(8,128)(4,1)S(1)} %broadcast_compare_fusion.4), kind=kOutput, calls=%fused_computation.179.clone.1 | convolution fusion | flops 477676640 | bytes 30971504 | tf_op jit(solution)/shard_map/while/body/eval_jaxpr/qhe,khe->hqk/dot_general | solution.py:143
  176.7 8.3 fusion.164
  198.2 9.8 fusion.162
  207.9 20.9 %fusion.163 = (f32[12,589]{1,0:T(8,128)S(1)}, f32[12,589,512]{2,1,0:T(8,128)}) fusion(f32[589,512,12]{1,2,0:T(8,128)} %fusion.162, bf16[589,12,64]{0,2,1:T(8,128)(2,1)S(1)} %bitcast.237, bf16[512,12,64]{0,2,1:T(8,128)(2,1)S(1)} %bitcast.241, pred[589,512]{1,0:T(8,128)(4,1)S(1)} %broadcast_compare_fusion.4), kind=kOutput, calls=%fused_computation.179.clone.1 | convolution fusion | flops 477676640 | bytes 30971504 | tf_op jit(solution)/shard_map/while/body/eval_jaxpr/qhe,khe->hqk/dot_general | solution.py:143
  228.9 8.5 fusion.164
  250.4 9.8 fusion.162
  260.2 21.0 %fusion.163 = (f32[12,589]{1,0:T(8,128)S(1)}, f32[12,589,512]{2,1,0:T(8,128)}) fusion(f32[589,512,12]{1,2,0:T(8,128)} %fusion.162, bf16[589,12,64]{0,2,1:T(8,128)(2,1)S(1)} %bitcast.237, bf16[512,12,64]{0,2,1:T(8,128)(2,1)S(1)} %bitcast.241, pred[589,512]{1,0:T(8,128)(4,1)S(1)} %broadcast_compare_fusion.4), kind=kOutput, calls=%fused_computation.179.clone.1 | convolution fusion | flops 477676640 | bytes 30971504 | tf_op jit(solution)/shard_map/while/body/eval_jaxpr/qhe,khe->hqk/dot_general | solution.py:143
  281.1 8.3 fusion.164
  303.7 17.8 %multiply_convert_fusion.3 = (bf16[3,589,3072]{2,1,0:T(8,128)(2,1)}, f32[3,589,3072]{2,1,0:T(8,128)}) fusion(f32[3072]{0:T(1024)S(1)} %copy-done.27, bf16[768,3072]{1,0:T(8,128)(2,1)} %all-gather.15.cloned.1.call-done, f32[3,589,768]{2,1,0:T(8,128)} %copy-done.3, f32[768]{0:T(1024)S(1)} %copy-done.28, f32[768]{0:T(1024)S(1)} %copy-done.24, ...), kind=kOutput, calls=%fused_computation.98 | convolution fusion | flops 8377106432 | bytes 42748728 | tf_op jit(solution)/shard_map/srd,de->sre/dot_general | solution.py:61
  321.6 13.7 %fusion.93 = (f32[3,589]{1,0:T(4,128)S(1)}, f32[3,589,768]{2,1,0:T(8,128)S(1)}) fusion(f32[768]{0:T(1024)S(1)} %copy-done.30, bf16[3,589,3072]{2,1,0:T(8,128)(2,1)} %get-tuple-element.359, bf16[3072,768]{1,0:T(8,128)(2,1)} %all-gather.17.cloned.1.call-done, f32[768]{0:T(1024)S(1)} %copy-done.28, f32[768]{0:T(1024)S(1)} %copy-done.24, ...), kind=kOutput, calls=%fused_computation.182 | convolution fusion | flops 8347249152 | bytes 26461908 | tf_op jit(solution)/shard_map/srd,de->sre/dot_general | solution.py:61
  345.0 20.8 %convert_reduce_fusion = (f32[3072]{0:T(1024)}, bf16[3,589,3072]{2,1,0:T(8,128)(2,1)}) fusion(f32[3,589,3072]{2,1,0:T(8,128)} %get-tuple-element.360, f32[3072]{0:T(1024)S(1)} %copy-done.27, bf16[3,589,768]{2,1,0:T(8,128)(2,1)S(1)} %get-tuple-element.339, bf16[3072,768]{1,0:T(8,128)(2,1)S(1)} %bitcast.251), kind=kOutput, calls=%fused_computation.97 | convolution fusion | flops 8408315904 | bytes 40026624 | tf_op jit(solution)/shard_map/sre,de->srd/dot_general | solution.py:65
  365.8 17.1 %multiply_reduce_fusion.1 = (f32[768]{0:T(1024)}, f32[3,589]{1,0:T(4,128)S(1)}, f32[768]{0:T(1024)}, f32[3,589,768]{2,1,0:T(8,128)}) fusion(f32[3,589,768]{2,1,0:T(8,128)S(1)} %bitcast.244, f32[3,589]{1,0:T(4,128)S(1)} %fusion.86, f32[3,589]{1,0:T(4,128)S(1)} %broadcast_multiply_fusion.1, f32[768]{0:T(1024)S(1)} %copy-done.24, ...), kind=kOutput, calls=%fused_computation.113 | convolution fusion | flops 8364889088 | bytes 34635588 | tf_op jit(solution)/shard_map/sre,de->srd/dot_general | solution.py:65
  396.2 5.9 convolution_convert_fusion
  404.0 239.7 %while.29 = (s32[]{:T(128)}, bf16[3,589,768]{1,2,0:T(8,128)(2,1)}, bf16[3,512,768]{1,2,0:T(8,128)(2,1)}, bf16[3,512,768]{1,2,0:T(8,128)(2,1)}, f32[3,32,12]{1,2,...) while((s32[]{:T(128)}, bf16[3,589,768]{1,2,0:T(8,128)(2,1)}, ...), condition=%wide.region_16.17_spmd, body=%wide.region_13.16_spmd.sunk | while | flops 2845565440 | bytes 232266512 | solution.py:265
  414.8 10.0 fusion.180
  424.8 18.8 %fusion.181 = f32[12,589,512]{2,1,0:T(8,128)} fusion(f32[589,512,12]{1,2,0:T(8,128)} %fusion.180, bf16[589,12,64]{0,2,1:T(8,128)(2,1)S(1)} %bitcast.230, bf16[512,12,64]{0,2,1:T(8,128)(2,1)S(1)} %bitcast.234, f32[12,589]{1,0:T(8,128)S(1)} %dynamic-slice_bitcast_fusion.8, pred[589,512]{1,0:T(8,128)(4,1)S(1)} %broadcast_compare_fusion.5), kind=kOutput, calls=%fused_computation.47.clone.1 | convolution fusion | flops 477683712 | bytes 30971504 | tf_op jit(solution)/shard_map/while/body/eval_jaxpr/qhe,khe->hqk/dot_general | solution.py:143
  443.5 7.7 fusion.182
  453.3 8.7 multiply_reduce_fusion.6
  461.9 6.7 multiply_convert_fusion.7
  468.7 9.6 fusion.183
  494.8 9.7 fusion.180
  504.5 18.7 %fusion.181 = f32[12,589,512]{2,1,0:T(8,128)} fusion(f32[589,512,12]{1,2,0:T(8,128)} %fusion.180, bf16[589,12,64]{0,2,1:T(8,128)(2,1)S(1)} %bitcast.230, bf16[512,12,64]{0,2,1:T(8,128)(2,1)S(1)} %bitcast.234, f32[12,589]{1,0:T(8,128)S(1)} %dynamic-slice_bitcast_fusion.8, pred[589,512]{1,0:T(8,128)(4,1)S(1)} %broadcast_compare_fusion.5), kind=kOutput, calls=%fused_computation.47.clone.1 | convolution fusion | flops 477683712 | bytes 30971504 | tf_op jit(solution)/shard_map/while/body/eval_jaxpr/qhe,khe->hqk/dot_general | solution.py:143
  523.3 7.6 fusion.182
  532.8 8.7 multiply_reduce_fusion.6
  541.5 6.7 multiply_convert_fusion.7
  548.2 9.6 fusion.183
  574.3 9.7 fusion.180
  584.0 18.7 %fusion.181 = f32[12,589,512]{2,1,0:T(8,128)} fusion(f32[589,512,12]{1,2,0:T(8,128)} %fusion.180, bf16[589,12,64]{0,2,1:T(8,128)(2,1)S(1)} %bitcast.230, bf16[512,12,64]{0,2,1:T(8,128)(2,1)S(1)} %bitcast.234, f32[12,589]{1,0:T(8,128)S(1)} %dynamic-slice_bitcast_fusion.8, pred[589,512]{1,0:T(8,128)(4,1)S(1)} %broadcast_compare_fusion.5), kind=kOutput, calls=%fused_computation.47.clone.1 | convolution fusion | flops 477683712 | bytes 30971504 | tf_op jit(solution)/shard_map/while/body/eval_jaxpr/qhe,khe->hqk/dot_general | solution.py:143
  602.7 7.6 fusion.182
  612.3 8.7 multiply_reduce_fusion.6
  620.9 6.7 multiply_convert_fusion.7
  627.7 9.6 fusion.183
  643.7 6.9 convolution_bitcast_fusion.3
  667.6 16.4 %convolution_bitcast_fusion.1 = f32[768,3072]{1,0:T(8,128)} fusion(bf16[3,589,3072]{2,1,0:T(8,128)(2,1)} %get-tuple-element.365, f32[3,589,768]{2,1,0:T(8,128)} %copy-done.3, f32[768]{0:T(1024)S(1)} %copy-done.29, f32[768]{0:T(1024)S(1)} %copy-done.25, f32[3,589]{1,0:T(4,128)S(1)} %copy-done.21, f32[3,589]{1,0:T(4,128)S(1)} %copy-done.17), kind=kOutput, calls=%fused_computation.109 | convolution fusion | flops 8344537088 | bytes 25742136 | tf_op jit(solution)/shard_map/srd,sre->de/dot_general | solution.py:69
  684.1 14.7 %convolution_bitcast_fusion = f32[3072,768]{1,0:T(8,128)} fusion(bf16[3,589,3072]{2,1,0:T(8,128)(2,1)} %get-tuple-element.359, bf16[3,589,768]{2,1,0:T(8,128)(2,1)} %copy-done.11), kind=kOutput, calls=%fused_computation.108 | convolution fusion | flops 8337752064 | bytes 23007744 | tf_op jit(solution)/shard_map/srd,sre->de/dot_general | solution.py:69
  704.0 6.1 fusion.77
  710.1 6.0 add_add_fusion.4
  719.2 59.6 %reduce-scatter.19.cloned.1.call-done = f32[48,768]{1,0:T(8,128)} async-done(((f32[768,768]{1,0:T(8,128)}), f32[48,768]{1,0:T(8,128)}) %reduce-scatter.19.cloned.1.call-update) | async-done | bytes 147472
  780.5 64.3 %reduce-scatter.21.cloned.1.call-done = f32[48,768]{1,0:T(8,128)} async-done(((f32[768,768]{1,0:T(8,128)}), f32[48,768]{1,0:T(8,128)}) %reduce-scatter.21.cloned.1.call-update) | async-done | bytes 147472
  846.6 112.8 %reduce-scatter.15.cloned.1.call-done = f32[48,3072]{1,0:T(8,128)} async-done(((f32[768,3072]{1,0:T(8,128)}), f32[48,3072]{1,0:T(8,128)}) %reduce-scatter.15.cloned.1.call-update) | async-done | bytes 589840 | tf_op jit(solution)/shard_map/reduce_scatter | solution.py:286
  961.2 113.8 %reduce-scatter.17.cloned.1.call-done = f32[192,768]{1,0:T(8,128)} async-done(((f32[3072,768]{1,0:T(8,128)}), f32[192,768]{1,0:T(8,128)}) %reduce-scatter.17.cloned.1.call-update) | async-done | bytes 589840 | tf_op jit(solution)/shard_map/reduce_scatter | solution.py:287
  1084.1 61.7 %all-reduce.20 = (bf16[768]{0:T(1024)(128)(2,1)S(1)}, bf16[768]{0:T(1024)(128)(2,1)S(1)}, bf16[768]{0:T(1024)(128)(2,1)S(1)}, bf16[768]{0:T(1024)(128)(2,1)}, bf...) all-reduce(f32[768]{0:T(1024)} %convert_reduce_fusion.2, ...), channel_id=8, replica_groups=mesh['dp'=2,'fsdp'=16] {'fsdp'}, use_global_device_ids=true, to_apply=%region_30.31.clone | all-reduce | flops 9600 | bytes 57600
  1154.3 5.7 all-reduce.22
  1173.7 8.0 fusion.62
  (345 shorter events, 244.3 us)
Async XLA Ops:
  7.2 87.3 %copy-start.12 = (bf16[3,512,768]{2,1,0:T(8,128)(2,1)S(1)}, bf16[3,512,768]{2,1,0:T(8,128)(2,1)}, u32[]{:S(2)}) copy-start(bf16[3,512,768]{2,1,0:T(8,128)(2,1)} %param.25) | copy-start | bytes 7077892
  7.2 86.5 %copy-start.15 = (bf16[3,77,768]{2,1,0:T(8,128)(2,1)S(1)}, bf16[3,77,768]{2,1,0:T(8,128)(2,1)}, u32[]{:S(2)}) copy-start(bf16[3,77,768]{2,1,0:T(8,128)(2,1)} %param.26) | copy-start | bytes 1064452
  7.2 87.3 %all-gather.7.cloned.1.call-start = ((), (), s32[]{:S(2)}) async-start(), calls=%async_computation.6 | async-start | bytes 1253376 | tf_op jit(solution)/shard_map/all_gather | solution.py:119
  7.9 95.6 %all-gather.11.cloned.1.call-start = ((), (), s32[]{:S(2)}) async-start(), calls=%async_computation.8 | async-start | bytes 1253376 | tf_op jit(solution)/shard_map/all_gather | solution.py:118
  8.7 122.3 %all-gather.9.cloned.1.call-start = ((), (), s32[]{:S(2)}) async-start(), calls=%async_computation.7 | async-start | bytes 1253376 | tf_op jit(solution)/shard_map/all_gather | solution.py:117
  9.4 286.2 %all-gather.13.cloned.1.call-start = ((), (), s32[]{:S(2)}) async-start(), calls=%async_computation.9 | async-start | bytes 1253376 | tf_op jit(solution)/shard_map/all_gather | solution.py:120
  10.0 293.6 %all-gather.15.cloned.1.call-start = ((), (), s32[]{:S(2)}) async-start(), calls=%async_computation.10 | async-start | bytes 5013504 | tf_op jit(solution)/shard_map/all_gather | solution.py:121
  10.6 310.9 %all-gather.17.cloned.1.call-start = ((), (), s32[]{:S(2)}) async-start(), calls=%async_computation.11 | async-start | bytes 5013504 | tf_op jit(solution)/shard_map/all_gather | solution.py:122
  11.2 704.9 %reduce-scatter.13.cloned.1.call-start = ((), (), s32[]{:S(2)}) async-start(), calls=%async_computation.13 | async-start | bytes 2506752 | tf_op jit(solution)/shard_map/reduce_scatter | solution.py:285
  135.4 3.6 copy-start.18
  139.0 156.7 %copy-start.31 = (f32[768]{0:T(1024)S(1)}, f32[768]{0:T(1024)}, u32[]{:S(2)}) copy-start(f32[768]{0:T(1024)} %convert_element_type.356) | copy-start | bytes 9220
  176.7 9.7 copy-start.1
  228.9 9.7 copy-start.1
  281.1 9.4 copy-start.1
  300.5 82.4 %copy-start.16 = (f32[3,589]{1,0:T(4,128)}, f32[3,589]{1,0:T(4,128)S(1)}, u32[]{:S(2)}) copy-start(f32[3,589]{1,0:T(4,128)S(1)} %broadcast_multiply_fusion.1) | copy-start | bytes 21208
  303.6 79.3 %copy-start.20 = (f32[3,589]{1,0:T(4,128)}, f32[3,589]{1,0:T(4,128)S(1)}, u32[]{:S(2)}) copy-start(f32[3,589]{1,0:T(4,128)S(1)} %fusion.86) | copy-start | bytes 21208
  303.6 17.9 %copy-start.30 = (f32[768]{0:T(1024)S(1)}, f32[768]{0:T(1024)}, u32[]{:S(2)}) copy-start(f32[768]{0:T(1024)} %convert_element_type.362) | copy-start | bytes 9220
  321.5 13.7 %copy-start.5 = (bf16[3,512,768]{2,1,0:T(8,128)(2,1)S(1)}, bf16[3,512,768]{2,1,0:T(8,128)(2,1)}, u32[]{:S(2)}) copy-start(bf16[3,512,768]{2,1,0:T(8,128)(2,1)} %param.44) | copy-start | bytes 7077892
  321.5 13.7 %copy-start.9 = (bf16[3,77,768]{2,1,0:T(8,128)(2,1)S(1)}, bf16[3,77,768]{2,1,0:T(8,128)(2,1)}, u32[]{:S(2)}) copy-start(bf16[3,77,768]{2,1,0:T(8,128)(2,1)} %param.45) | copy-start | bytes 1064452
  321.5 13.7 %copy-start.19 = (f32[768]{0:T(1024)S(1)}, f32[768]{0:T(1024)}, u32[]{:S(2)}) copy-start(f32[768]{0:T(1024)} %convert_element_type.363) | copy-start | bytes 9220
  337.2 3.6 copy-start.26
  337.2 7.8 slice-start.4
  340.8 4.2 slice-start.5
  340.8 25.0 %slice-start = ((s8[5455872]{0:T(1024)(128)(4,1)}), s8[4194304]{0:T(1024)(128)(4,1)S(1)}, s32[]{:S(2)}) async-start(s8[5455872]{0:T(1024)(128)(4,1)} %bitcast.243), calls=%async_computation.19 | async-start | bytes 8388608
  345.0 20.8 %copy-start.11 = (bf16[3,589,768]{2,1,0:T(8,128)(2,1)}, bf16[3,589,768]{2,1,0:T(8,128)(2,1)S(1)}, u32[]{:S(2)}) copy-start(bf16[3,589,768]{2,1,0:T(8,128)(2,1)S(1)} %get-tuple-element.339) | copy-start | bytes 8142340
  345.0 20.8 %slice-start.1 = ((s8[5455872]{0:T(1024)(128)(4,1)}), s8[1261568]{0:T(1024)(128)(4,1)S(1)}, s32[]{:S(2)}) async-start(s8[5455872]{0:T(1024)(128)(4,1)} %bitcast.243), calls=%async_computation.20 | async-start | bytes 2523136
  387.4 8.8 copy-start.22
  396.2 321.5 %reduce-scatter.11.cloned.1.call-start = ((), (), s32[]{:S(2)}) async-start(), calls=%async_computation.12 | async-start | bytes 2506752 | tf_op jit(solution)/shard_map/reduce_scatter | solution.py:282
  443.5 9.7 copy-start
  479.7 3.3 copy-start.2
  523.3 9.6 copy-start
  602.7 9.6 copy-start
  643.7 7.0 copy-start.13
  650.6 128.1 %reduce-scatter.19.cloned.1.call-start = ((), (), s32[]{:S(2)}) async-start(), calls=%async_computation.16 | async-start | bytes 2506752
  655.8 3.3 copy-start.6
  659.0 185.8 %reduce-scatter.21.cloned.1.call-start = ((), (), s32[]{:S(2)}) async-start(), calls=%async_computation.17 | async-start | bytes 2506752
  664.3 3.3 copy-start.25
  664.3 3.3 copy-start.29
  667.5 291.9 %reduce-scatter.15.cloned.1.call-start = ((), (), s32[]{:S(2)}) async-start(), calls=%async_computation.14 | async-start | bytes 10027008 | tf_op jit(solution)/shard_map/reduce_scatter | solution.py:286
  684.0 391.0 %reduce-scatter.17.cloned.1.call-start = ((), (), s32[]{:S(2)}) async-start(), calls=%async_computation.15 | async-start | bytes 10027008 | tf_op jit(solution)/shard_map/reduce_scatter | solution.py:287
  698.8 5.2 copy-start.32
  698.8 482.9 %all-reduce.26.cloned.1.call-start = ((), (), s32[]{:S(2)}) async-start(), calls=%async_computation.18 | async-start | bytes 2260992 | tf_op jit(solution)/shard_map/psum | solution.py:300
  700.9 9.2 slice-start.2
  704.0 6.1 slice-start.3
  704.0 6.1 copy-start.7
  704.0 6.1 copy-start.23
  704.0 6.1 copy-start.33
  1076.8 96.9 %copy-start.14 = (bf16[768,768]{1,0:T(8,128)(2,1)S(1)}, bf16[768,768]{1,0:T(8,128)(2,1)}, u32[]{:S(2)}) copy-start(bf16[768,768]{1,0:T(8,128)(2,1)} %all-gather.7.cloned.1.call-done) | copy-start | bytes 3538948
  (11 other events, 32.1 us)
Sparse Core Ops, SparseCore 0:
  10.3 41.0 all-gather.6
  53.7 37.4 all-gather.10
  93.5 37.4 all-gather.8
  133.1 37.2 all-gather.12
  172.6 52.1 all-gather.14
  226.9 51.7 all-gather.16
  396.3 62.0 reduce-scatter.12
  650.8 62.2 reduce-scatter.10
  716.8 61.9 reduce-scatter.18
  782.9 61.9 reduce-scatter.20
  848.9 110.3 reduce-scatter.14
  963.9 111.0 reduce-scatter.16
  1078.8 42.4 all-reduce.25
where the time goes:
time: 1210 us; the launch traced here: 1200 us
  matrix products  446 us (37%)
  waiting for transfers between devices  373 us (31%)
  blocking collectives  131 us (11%)
  local copies, waits for them, and re-layouts  123 us (10%)
  other arithmetic  105 us (9%)
  between operations  18.7 us (2%)
    unnamed x15, waiting for transfers between devices  128 us
    unnamed x2, blocking collectives  125 us
    dot_general x6, matrix products, scores_of(): jnp.einsum('qhe,khe->hqk', query_rows.reshape(row_count, HEADS, HEAD), ke...  119 us
    reduce_scatter x1, waiting for transfers between devices, per_device(): lax.psum_scatter(outer_weight_grad, 'fsdp', scatter_dimension=0, tiled=True)  114 us
    reduce_scatter x1, waiting for transfers between devices, per_device(): lax.psum_scatter(inner_weight_grad, 'fsdp', scatter_dimension=0, tiled=True)  113 us
    dot_general x6, matrix products, project_back(): jnp.einsum('sre,de->srd', left, right_matrix, preferred_element_type=jnp....  63.8 us
    dot_general x6, matrix products, scores_of(): jnp.einsum('qkb,bh->hqk', onehot, bucket_table, preferred_element_type=jn...  58.7 us
    dot_general x6, matrix products, outer_sum(): jnp.einsum('srd,sre->de', left, right_rows, preferred_element_type=jnp.fl...  52.1 us
  transfers between devices with their start and end apart: 13, of which 5 were waited for; matrix products, arithmetic and copies ran while one was open for 48% of the time, Pallas kernels for 0%

commit v1 on v0

v1 whole, which is shorter than its diff:
```python
import functools

import jax
import jax.numpy as jnp
from jax import lax
from jax.experimental import pallas as pl
from jax.experimental.pallas import tpu as pltpu
from jax.sharding import PartitionSpec as P

D = 768
HEADS = 12
HEAD = 64
BUCKETS = 32
LEN = 512
PRED = 77
QP = 80
R = LEN + QP
f32 = jnp.float32
bf16 = jnp.bfloat16
NT = (((1,), (1,)), ((), ()))

eps_norm = 1e-05
inverse_root = 0.7071067811865476
density_scale = 0.3989422804014327
bucket_edges = (12, 16, 23, 32, 46, 64, 91)
VMEM_LIMIT = 60 * 1024 * 1024


def bucket_index(relative):
    distance = jnp.abs(relative)
    coarse = 8 + sum(((distance >= boundary).astype(jnp.int32) for boundary in bucket_edges))
    within = jnp.where(distance < 8, distance, coarse)
    return within + 16 * (relative > 0).astype(jnp.int32)


def iota(shape, dim):
    return lax.broadcasted_iota(jnp.int32, shape, dim)


def ranking_column(perm_row):
    hit = perm_row == iota((LEN, LEN), 0)
    return jnp.sum(jnp.where(hit, iota((LEN, LEN), 1), 0).astype(f32), axis=1, keepdims=True)


def build_bias(table, full, near, far):
    rel = iota((128, 1024), 1) - 512
    onehot = (bucket_index(rel) == iota((128, 1024), 0)).astype(bf16)
    by_rel = jnp.dot(table, onehot, preferred_element_type=f32)
    for h in range(HEADS):
        far[h, 0:8] = jnp.broadcast_to(by_rel[h : h + 1, 0:1], (8, 128))
        far[h, 8:16] = jnp.broadcast_to(by_rel[h : h + 1, 1023:1024], (8, 128))
        for d in range(-3, 4):
            if abs(d) >= 2:
                at = 512 + 128 * d
                block = jnp.broadcast_to(by_rel[h : h + 1, at : at + 1], (128, 128)).astype(bf16)
            else:
                base = 512 + 128 * d - 128
                row = jnp.broadcast_to(by_rel[h : h + 1, base : base + 256], (128, 256))
                tile = pltpu.roll(row, 0, 1, stride=1, stride_axis=0)[:, 128:]
                near[h, d + 1] = tile
                block = tile.astype(bf16)
            for bi in range(4):
                bj = bi + d
                if 0 <= bj < 4:
                    full[h, bi * 128 : (bi + 1) * 128, bj * 128 : (bj + 1) * 128] = block


def attn_fwd(
    perm_ref, x_ref, wq, wk, wv, bq, bv, tab_ref,
    q_ref, k_ref, v_ref, o_ref, ol_ref, r_ref, p_ref,
    full, near, far, scores, row_mark, key_mark, slot_hot,
):
    s = pl.program_id(0)
    hp = pl.program_id(1)

    @pl.when((s == 0) & (hp == 0))
    def _():
        build_bias(tab_ref[...], full, near, far)

    @pl.when(hp == 0)
    def _():
        x = x_ref[0]
        q = (jnp.dot(x, wq[...], preferred_element_type=f32) + bq[...]).astype(bf16)
        q_ref[0] = q * jnp.asarray(0.125, bf16)
        xc = x[:LEN]
        k_ref[0] = jnp.dot(xc, wk[...], preferred_element_type=f32).astype(bf16)
        v_ref[0] = (jnp.dot(xc, wv[...], preferred_element_type=f32) + bv[...]).astype(bf16)
        rank = ranking_column(perm_ref[0])
        rank_row = jnp.transpose(jnp.broadcast_to(rank, (LEN, 128)))[:1]
        slot = iota((LEN, 128), 1).astype(f32) + float(LEN - PRED)
        limit = jnp.maximum(rank, float(LEN - PRED - 1))
        row_mark[:LEN] = jnp.where(limit < slot, 1.0, 0.0).astype(bf16)
        row_mark[LEN:] = jnp.where(iota((QP, 128), 0) <= iota((QP, 128), 1), 1.0, 0.0).astype(bf16)
        key_mark[...] = jnp.where(rank == slot, -1e9, 0.0).astype(bf16)
        wanted = (iota((QP, LEN), 0) + (LEN - PRED)).astype(f32)
        slot_hot[...] = (rank_row == wanted).astype(bf16)

    cols = pl.ds(pl.multiple_of(hp * 128, 128), 128)
    q2 = q_ref[0, :, cols]
    k2 = k_ref[0, :, cols]
    v2 = v_ref[0, :, cols]
    half = iota((LEN, 128), 1) // 64
    left = jnp.concatenate([q2, row_mark[...]], axis=1)
    for h in range(2):
        right = jnp.concatenate([jnp.where(half == h, k2, jnp.zeros_like(k2)), key_mark[...]], axis=1)
        scores[h, :LEN] = lax.dot_general(left[:LEN], right, NT, preferred_element_type=f32)
        scores[h, LEN:] = lax.dot_general(left[LEN:], right, NT, preferred_element_type=f32) + jnp.dot(
            slot_hot[...], full[2 * hp + h], preferred_element_type=f32
        )
    for h in range(2):
        head = 2 * hp + h
        for bi in range(4):
            rows = slice(bi * 128, bi * 128 + 128)
            tiles = []
            for bj in range(4):
                d = bj - bi
                bias = near[head, d + 1] if abs(d) < 2 else far[head, 8:9] if d > 0 else far[head, 0:1]
                tiles.append(scores[h, rows, bj * 128 : (bj + 1) * 128] + bias)
            biased = jnp.concatenate(tiles, axis=1)
            peak = jnp.max(biased, axis=1, keepdims=True)
            p_ref[0, h, rows] = jnp.exp(biased - peak).astype(bf16)
        biased = scores[h, LEN:]
        peak = jnp.max(biased, axis=1, keepdims=True)
        p_ref[0, h, LEN:] = jnp.exp(biased - peak).astype(bf16)
    mixed = []
    for h in range(2):
        vm = jnp.where(half == h, v2, jnp.ones_like(v2))
        mixed.append(jnp.dot(p_ref[0, h], vm, preferred_element_type=f32))
    low = iota((R, 128), 1) < 64
    inverse = 1.0 / pltpu.roll(jnp.where(low, mixed[1], mixed[0]), 64, 1)
    out = jnp.where(low, mixed[0], mixed[1]) * inverse
    out_low = out.astype(bf16)
    o_ref[0, :, cols] = out_low
    ol_ref[0, :, cols] = (out - out_low.astype(f32)).astype(bf16)
    r_ref[0, :, cols] = inverse


def whole_rows(n):
    return pl.BlockSpec((1, n, D), lambda s, h: (s, 0, 0))


def fixed(shape):
    return pl.BlockSpec(shape, lambda s, h: (0,) * len(shape))


def attention_forward(perm, x, wq, wk, wv, bq, bv, table):
    n = x.shape[0]
    sds = jax.ShapeDtypeStruct
    return pl.pallas_call(
        attn_fwd,
        grid=(n, HEADS // 2),
        in_specs=[pl.BlockSpec((1, 1, LEN), lambda s, h: (s, 0, 0)), whole_rows(R)]
        + [fixed((D, D))] * 3
        + [fixed((1, D))] * 2
        + [fixed((16, 128))],
        out_specs=[
            whole_rows(R), whole_rows(LEN), whole_rows(LEN), whole_rows(R), whole_rows(R), whole_rows(R),
            pl.BlockSpec((1, 2, R, LEN), lambda s, h: (s, h, 0, 0)),
        ],
        out_shape=[
            sds((n, R, D), bf16), sds((n, LEN, D), bf16), sds((n, LEN, D), bf16), sds((n, R, D), bf16),
            sds((n, R, D), bf16), sds((n, R, D), f32), sds((n, HEADS, R, LEN), bf16),
        ],
        scratch_shapes=[
            pltpu.VMEM((HEADS, LEN, LEN), bf16),
            pltpu.VMEM((HEADS, 3, 128, 128), f32),
            pltpu.VMEM((HEADS, 16, 128), f32),
            pltpu.VMEM((2, R, LEN), f32),
            pltpu.VMEM((R, 128), bf16),
            pltpu.VMEM((LEN, 128), bf16),
            pltpu.VMEM((QP, LEN), bf16),
        ],
        compiler_params=pltpu.CompilerParams(vmem_limit_bytes=VMEM_LIMIT),
        name="attention_forward",
    )(perm[:, None], x, wq, wk, wv, bq, bv, table)


def reduce_table(n, slot_cols, kept, near_sum, far_sum):
    c = iota((896, 128), 0)
    rel = jnp.where(c < 768, 128 * (c // 256 - 1) + c % 256 - 128, jnp.where(c % 128 < 64, -200, 200))
    onehot = (bucket_index(rel) == iota((896, 128), 1)).astype(f32)
    slots = jnp.concatenate([slot_cols[i] for i in range(n)], axis=1)
    sub = iota((8, 256), 0)
    lane8 = iota((8, 128), 1)
    lane1 = iota((1, 128), 1)
    rows = []
    for head in range(HEADS):
        moved = jnp.dot(slots, kept[head], preferred_element_type=f32)
        near = [near_sum[head, d] for d in range(3)]
        far = [far_sum[head, 0:8], far_sum[head, 8:16]]
        for bi in range(4):
            for bj in range(4):
                d = bj - bi
                tile = moved[bi * 128 : (bi + 1) * 128, bj * 128 : (bj + 1) * 128]
                if abs(d) < 2:
                    near[d + 1] = near[d + 1] + tile
                else:
                    far[int(d > 0)] = far[int(d > 0)] + tile.reshape(16, 8, 128).sum(0)
        parts = []
        for d in range(3):
            high = low = None
            for a in range(16):
                x = near[d][8 * a : 8 * a + 8]
                if a:
                    x = pltpu.roll(x, 128 - 8 * a, 1)
                keep = lane8 < 128 - 8 * a
                u = jnp.where(keep, x, 0.0)
                w = jnp.where(keep, 0.0, x)
                high = u if high is None else high + u
                low = w if low is None else low + w
            y = jnp.concatenate([low, high], axis=1)
            for k in (1, 2, 4):
                y = jnp.where((sub & k) != 0, pltpu.roll(y, 256 - k, 1), y)
            parts.append(jnp.sum(y, axis=0, keepdims=True))
        parts.append(jnp.where(lane1 == 0, jnp.sum(far[0]), jnp.where(lane1 == 64, jnp.sum(far[1]), 0.0)))
        rows.append(jnp.concatenate(parts, axis=1))
    rows.append(jnp.zeros((4, 896), f32))
    return jnp.dot(
        jnp.concatenate(rows, axis=0), onehot, preferred_element_type=f32, precision=lax.Precision.HIGHEST
    )


def attn_bwd(
    perm_ref, q_ref, k_ref, v_ref, o_ref, ol_ref, r_ref, p_ref, do_ref,
    dq_ref, dk_ref, dv_ref, tab_ref,
    dp, ds, kept, slot_cols, near_sum, far_sum,
):
    n = slot_cols.shape[0]
    s = pl.program_id(0)
    hp = pl.program_id(1)

    @pl.when((s == 0) & (hp == 0))
    def _():
        near_sum[...] = jnp.zeros_like(near_sum)
        far_sum[...] = jnp.zeros_like(far_sum)

    @pl.when(hp == 0)
    def _():
        rank = ranking_column(perm_ref[0])
        slot_cols[s] = (rank == (iota((LEN, QP), 1) + (LEN - PRED)).astype(f32)).astype(bf16)

    cols = pl.ds(pl.multiple_of(hp * 128, 128), 128)
    q2 = q_ref[0, :, cols]
    k2 = k_ref[0, :, cols]
    v2 = v_ref[0, :, cols]
    delta = (do_ref[0, :, cols].astype(f32) * r_ref[0, :, cols]).astype(bf16)
    prod = delta.astype(f32) * (o_ref[0, :, cols].astype(f32) + ol_ref[0, :, cols].astype(f32))
    high = prod.astype(bf16)
    rest = pltpu.roll(prod - high.astype(f32), 64, 1).astype(bf16)
    low = iota((R, 128), 1) < 64
    half = iota((LEN, 128), 1) // 64
    extra = [jnp.where(low, high, rest), jnp.where(low, rest, high)]
    minus = jnp.full((LEN, 128), -1.0, bf16)
    for h in range(2):
        vm = jnp.where(half == h, v2, jnp.zeros_like(v2))
        dp[h] = lax.dot_general(
            jnp.concatenate([delta, extra[h]], axis=1),
            jnp.concatenate([vm, minus], axis=1),
            NT,
            preferred_element_type=f32,
        )
    for h in range(2):
        head = 2 * hp + h
        far = [None, None]
        for bi in range(4):
            rows = slice(bi * 128, bi * 128 + 128)
            d_rows = p_ref[0, h, rows].astype(f32) * dp[h, rows]
            ds[h, rows] = d_rows.astype(bf16)
            for bj in range(4):
                d = bj - bi
                tile = d_rows[:, bj * 128 : (bj + 1) * 128]
                if abs(d) < 2:
                    near_sum[head, d + 1] += tile
                else:
                    part = tile.reshape(16, 8, 128).sum(0)
                    far[int(d > 0)] = part if far[int(d > 0)] is None else far[int(d > 0)] + part
        far_sum[head, 0:8] += far[0]
        far_sum[head, 8:16] += far[1]
        d_slots = (p_ref[0, h, LEN:].astype(f32) * dp[h, LEN:]).astype(bf16)
        ds[h, LEN:] = d_slots
        kept[head, pl.ds(pl.multiple_of(s * QP, 16), QP)] = d_slots
    dq = None
    for h in range(2):
        km = jnp.where(half == h, k2, jnp.zeros_like(k2))
        part = jnp.dot(ds[h], km, preferred_element_type=f32)
        dq = part if dq is None else dq + part
    dq_ref[0, :, cols] = (dq * 0.125).astype(bf16)
    q_t = jnp.transpose(q2)
    delta_t = jnp.transpose(delta)
    dk_t = [jnp.dot(q_t[h * 64 : (h + 1) * 64], ds[h], preferred_element_type=f32) for h in range(2)]
    dv_t = [jnp.dot(delta_t[h * 64 : (h + 1) * 64], p_ref[0, h], preferred_element_type=f32) for h in range(2)]
    dk_ref[0, :, cols] = jnp.transpose(jnp.concatenate(dk_t, axis=0).astype(bf16))
    dv_ref[0, :, cols] = jnp.transpose(jnp.concatenate(dv_t, axis=0).astype(bf16))

    @pl.when((s == n - 1) & (hp == HEADS // 2 - 1))
    def _():
        tab_ref[...] = reduce_table(n, slot_cols, kept, near_sum, far_sum)


def attention_backward(perm, q, k, v, o, ol, r, p, do):
    n = q.shape[0]
    sds = jax.ShapeDtypeStruct
    return pl.pallas_call(
        attn_bwd,
        grid=(n, HEADS // 2),
        in_specs=[
            pl.BlockSpec((1, 1, LEN), lambda s, h: (s, 0, 0)),
            whole_rows(R), whole_rows(LEN), whole_rows(LEN), whole_rows(R), whole_rows(R), whole_rows(R),
            pl.BlockSpec((1, 2, R, LEN), lambda s, h: (s, h, 0, 0)),
            whole_rows(R),
        ],
        out_specs=[whole_rows(R), whole_rows(LEN), whole_rows(LEN), fixed((16, 128))],
        out_shape=[sds((n, R, D), bf16), sds((n, LEN, D), bf16), sds((n, LEN, D), bf16), sds((16, 128), f32)],
        scratch_shapes=[
            pltpu.VMEM((2, R, LEN), f32),
            pltpu.VMEM((2, R, LEN), bf16),
            pltpu.VMEM((HEADS, n * QP, LEN), bf16),
            pltpu.VMEM((n, LEN, QP), bf16),
            pltpu.VMEM((HEADS, 3, 128, 128), f32),
            pltpu.VMEM((HEADS, 16, 128), f32),
        ],
        compiler_params=pltpu.CompilerParams(vmem_limit_bytes=VMEM_LIMIT),
        name="attention_backward",
    )(perm[:, None], q, k, v, o, ol, r, p, do)


def norm_parts(values):
    centered = values - jnp.mean(values, axis=-1, keepdims=True)
    inv = lax.rsqrt(jnp.mean(centered * centered, axis=-1, keepdims=True) + eps_norm)
    return centered * inv, inv


def norm_back(grad, unit, inv, gain):
    scaled = grad * gain
    return inv * (
        scaled - jnp.mean(scaled, axis=-1, keepdims=True) - unit * jnp.mean(scaled * unit, axis=-1, keepdims=True)
    )


def gelu_slope(values):
    return 0.5 * (1.0 + lax.erf(values * inverse_root)) + values * jnp.exp(-0.5 * values * values) * density_scale


def project(left, right_matrix):
    return jnp.einsum("srd,de->sre", left, right_matrix, preferred_element_type=f32)


def project_back(left, right_matrix):
    return jnp.einsum("sre,de->srd", left, right_matrix, preferred_element_type=f32)


def outer_sum(left, right_rows):
    return jnp.einsum("srd,sre->de", left, right_rows, preferred_element_type=f32)


def row_sum(values):
    return jnp.sum(values.astype(f32), axis=(0, 1))


def per_device(
    content_in, query_in, permutation,
    query_weight, key_weight, value_weight, output_weight, inner_weight, outer_weight,
    query_bias, value_bias, output_bias, first_gain, first_shift, inner_bias, outer_bias,
    second_gain, second_shift, bias_table,
    content_cotangent, query_cotangent,
):
    own = query_weight.shape[0]
    n_f = lax.axis_size("fsdp")
    vectors = (
        query_bias, value_bias, output_bias, first_gain, first_shift, outer_bias, second_gain, second_shift,
        inner_bias, bias_table,
    )
    sizes = [a.shape[0] for a in vectors]

    def gather(a):
        return lax.all_gather(a, "fsdp", axis=0, tiled=True)

    packed = lax.all_gather(jnp.concatenate(vectors), "fsdp", axis=0)
    full_vectors = []
    at = 0
    for size in sizes:
        full_vectors.append(packed[:, at : at + size].reshape(-1).astype(f32))
        at += size
    bq, bv, bo, g1, s1, b2, g2, s2, b1, table_flat = full_vectors
    table = jnp.zeros((16, 128), bf16).at[:HEADS, :BUCKETS].set(
        table_flat.reshape(BUCKETS, HEADS).T.astype(bf16)
    )
    qkvo = gather(jnp.concatenate([query_weight, key_weight, value_weight, output_weight], axis=1))
    wq, wk, wv, wo = (qkvo[:, i * D : (i + 1) * D] for i in range(4))
    w1 = gather(inner_weight)
    w2 = gather(outer_weight)

    pad = ((0, 0), (0, QP - PRED), (0, 0))
    x = jnp.concatenate([content_in, jnp.pad(query_in, pad)], axis=1)
    cot = jnp.concatenate([content_cotangent, jnp.pad(query_cotangent, pad)], axis=1).astype(f32)

    q, k, v, o, ol, r, p = attention_forward(permutation, x, wq, wk, wv, bq[None], bv[None], table)

    y1 = x.astype(f32) + project(o, wo) + bo
    unit1, inv1 = norm_parts(y1)
    normed = unit1 * g1 + s1
    low1 = normed.astype(bf16)
    hidden = project(low1, w1) + b1
    act = (0.5 * hidden * (1.0 + lax.erf(hidden * inverse_root))).astype(bf16)
    y2 = normed + project(act, w2) + b2
    unit2, inv2 = norm_parts(y2)
    out = (unit2 * g2 + s2).astype(bf16)

    s2_grad = row_sum(cot)
    g2_grad = row_sum(cot * unit2)
    back2 = norm_back(cot, unit2, inv2, g2)
    d2 = back2.astype(bf16)
    b2_grad = row_sum(d2)
    w2_grad = outer_sum(act, d2)
    dh = (project_back(d2, w2) * gelu_slope(hidden)).astype(bf16)
    b1_grad = row_sum(dh)
    w1_grad = outer_sum(low1, dh)
    da = back2 + project_back(dh, w1)
    s1_grad = row_sum(da)
    g1_grad = row_sum(da * unit1)
    back1 = norm_back(da, unit1, inv1, g1)
    d1 = back1.astype(bf16)
    bo_grad = row_sum(d1)
    wo_grad = outer_sum(o, d1)
    do = project_back(d1, wo).astype(bf16)

    dq, dk, dv, table_grad = attention_backward(permutation, q, k, v, o, ol, r, p, do)

    wq_grad = outer_sum(x, dq)
    wk_grad = outer_sum(x[:, :LEN], dk)
    wv_grad = outer_sum(x[:, :LEN], dv)
    bq_grad = row_sum(dq)
    bv_grad = row_sum(dv)
    dx = back1 + project_back(dq, wq)
    content_grad = dx[:, :LEN] + project_back(dk, wk) + project_back(dv, wv)
    query_grad = dx[:, LEN : LEN + PRED]

    def scatter(a):
        return lax.psum_scatter(a.astype(bf16), "fsdp", scatter_dimension=0, tiled=True)

    qkvo_grad = scatter(jnp.concatenate([wq_grad, wk_grad, wv_grad, wo_grad], axis=1))
    w1_share = scatter(w1_grad)
    w2_share = scatter(w2_grad)
    table_grad_flat = table_grad[:HEADS, :BUCKETS].T.reshape(-1)
    vector_grads = (bq_grad, bv_grad, bo_grad, g1_grad, s1_grad, b2_grad, g2_grad, s2_grad, b1_grad, table_grad_flat)
    packed_grads = jnp.concatenate([a.reshape(n_f, -1) for a in vector_grads], axis=1)
    packed_share = lax.psum_scatter(packed_grads, "fsdp", scatter_dimension=0, tiled=True).astype(bf16)
    qkvo_grad, w1_share, w2_share, packed_share = jax.tree.map(
        lambda a: a.astype(f32), lax.psum((qkvo_grad, w1_share, w2_share, packed_share), "dp")
    )
    parts = []
    at = 0
    for size in sizes:
        parts.append(packed_share[0, at : at + size])
        at += size
    bq_s, bv_s, bo_s, g1_s, s1_s, b2_s, g2_s, s2_s, b1_s, tab_s = parts
    wq_s, wk_s, wv_s, wo_s = (qkvo_grad[:, i * D : (i + 1) * D] for i in range(4))
    return (
        out[:, :LEN], out[:, LEN : LEN + PRED], content_grad, query_grad,
        wq_s, wk_s, wv_s, wo_s, w1_share, w2_share,
        bq_s, bv_s, bo_s, g1_s, s1_s, b1_s, b2_s, g2_s, s2_s, tab_s,
    )


def solution(mesh):
    rows3 = P(("dp", "fsdp"), None, None)
    matrix = P("fsdp", None)
    vector = P("fsdp")
    return jax.shard_map(
        per_device,
        mesh=mesh,
        in_specs=(rows3, rows3, P(("dp", "fsdp"), None)) + (matrix,) * 6 + (vector,) * 10 + (rows3, rows3),
        out_specs=(rows3,) * 4 + (matrix,) * 6 + (vector,) * 10,
        check_vma=False,
    )
```

time: 1210 us -> 607 us (0.50)
  matrix products: 446 us -> 140 us
  waiting for transfers between devices: 373 us -> 162 us
  Pallas kernels: 0 us -> 83.1 us
  local copies, waits for them, and re-layouts: 123 us -> 42.8 us
  other arithmetic: 105 us -> 25.6 us
    dot_general x48 -> x15, matrix products: 446 us -> 140 us  [the longest x6 62.9 us: project_back(): jnp.einsum('sre,de->srd', left, right_matrix, preferred_element_type=f32)]
    unnamed x15 -> x8, waiting for transfers between devices: 128 us -> 1.46 us
    reduce_scatter x4 -> x2, waiting for transfers between devices: 227 us -> 113 us  [scatter(): lax.psum_scatter(a.astype(bf16), 'fsdp', scatter_dimension=0, tiled=True)]
    pallas_call x0 -> x2, Pallas kernels: none -> 83.1 us  [the longest x1 42 us: attention_forward(): pl.pallas_call(attn_fwd, grid=(n, HEADS // 2), in_specs=[pl.BlockSpec((1,...]
    convert_element_type x30 -> x5, other arithmetic: 49.5 us -> 1.8 us  [the longest x3 1.72 us: per_device(): a.astype(f32)]
    psum x1, waiting for transfers between devices: 0.01 us -> 34.6 us  [per_device(): lax.psum((qkvo_grad, w1_share, w2_share, packed_share), 'dp')]
    reduce_sum x12 -> x7, other arithmetic: 46.5 us -> 16 us  [the longest x5 14.6 us: row_sum(): return jnp.sum(values.astype(f32), axis=(0, 1))]
    dynamic_slice x21 -> x0, local copies, waits for them, and re-layouts: 27.7 us -> none  [per_device(): lax.map(attend, (queries, keys_all, values_all, permutation))]
  transfers between devices with their start and end apart: 13 -> 7, of which waited for: 5 -> 4; matrix products, arithmetic and copies ran while one was open for 48% -> 18% of each run, Pallas kernels for 0% -> 7%
where the time goes in v1:
time: 607 us; the launch traced here: 599 us
  waiting for transfers between devices  162 us (27%)
  matrix products  140 us (23%)
  blocking collectives  130 us (21%)
  Pallas kernels  83.1 us (14%)
  local copies, waits for them, and re-layouts  42.8 us (7%)
  other arithmetic  25.6 us (4%)
  between operations  15.6 us (3%)
    unnamed x2, blocking collectives  125 us
    reduce_scatter x2, waiting for transfers between devices, scatter(): lax.psum_scatter(a.astype(bf16), 'fsdp', scatter_dimension=0, tiled=True)  113 us
    dot_general x6, matrix products, project_back(): jnp.einsum('sre,de->srd', left, right_matrix, preferred_element_type=f32)  62.9 us
    pallas_call x1, Pallas kernels, attention_forward(): pl.pallas_call(attn_fwd, grid=(n, HEADS // 2), in_specs=[pl.BlockSpec((1,...  42 us
    pallas_call x1, Pallas kernels, attention_backward(): pl.pallas_call(attn_bwd, grid=(n, HEADS // 2), in_specs=[pl.BlockSpec((1,...  41.1 us
    dot_general x6, matrix products, outer_sum(): jnp.einsum('srd,sre->de', left, right_rows, preferred_element_type=f32)  40.5 us
    dot_general x3, matrix products, project(): jnp.einsum('srd,de->sre', left, right_matrix, preferred_element_type=f32)  36.3 us
    psum x1, waiting for transfers between devices, per_device(): lax.psum((qkvo_grad, w1_share, w2_share, packed_share), 'dp')  34.6 us
  transfers between devices with their start and end apart: 7, of which 4 were waited for; matrix products, arithmetic and copies ran while one was open for 18% of the time, Pallas kernels for 7%

profile of v1, /device:TPU:0, one launch (start us, length us, event | category | flops | bytes accessed | tf_op | source)
XLA Modules:
  0.0 598.9 jit_solution(1914850426458699221)
XLA Ops:
  7.2 1.7 pad_maximum_fusion.1
  10.5 1.3 fusion.49
  12.5 6.8 %concatenate.23 = bf16[600]{0:T(1024)(128)(2,1)S(1)} concatenate(bf16[48]{0:T(256)(128)(2,1)} %param.32, bf16[48]{0:T(256)(128)(2,1)} %param.33, bf16[48]{0:T(256)(128)(2,1)} %param.34, bf16[48]{0:T(256)(128)(2,1)} %param.35, bf16[48]{0:T(256)(128)(2,1)} %param.36, bf16[48]{0:T(256)(128)(2,1)} %param.38, bf16[48]{0:T(256)(128)(2,1)} %param.39, bf16[48]{0:T(256)(128)(2,1)} %param.40, ...), dimensions={0} | concatenate | bytes 2400 | tf_op jit(solution)/shard_map/concatenate | solution.py:378
  19.5 63.8 %all-reduce.3 = bf16[9600]{0:T(1024)(128)(2,1)S(1)} all-reduce(bf16[9600]{0:T(1024)(128)(2,1)S(1)} %dynamic-update-slice.2), channel_id=2, replica_groups=mesh['dp'=2,'fsdp'=16] {'fsdp'}, use_global_device_ids=true, to_apply=%add.3 | all-reduce | flops 9600 | bytes 38400
  83.8 1.3 broadcast_in_dim.2.perm_ref
  87.5 3.5 fusion.24.x_ref
  91.1 4.1 fusion.47
  95.1 42.0 %attention_forward.1 = (bf16[3,592,768]{2,1,0:T(8,128)(2,1)}, bf16[3,512,768]{2,1,0:T(8,128)(2,1)}, bf16[3,512,768]{2,1,0:T(8,128)(2,1)}, bf16[3,592,768]{2,1,0:...) custom-call(s32[3,1,512]{2,1,0:T(1,128)} %broadcast_in_dim.2.perm_ref, ...), custom_call_target="tpu_custom_call" | custom-call | tf_op jit(solution)/shard_map/attention_forward/pallas_call | solution.py:149
  137.1 4.7 fusion.50
  141.8 2.3 copy-done
  144.9 17.6 %multiply_convert_fusion = (bf16[3,592,3072]{2,1,0:T(8,128)(2,1)}, f32[3,592,3072]{2,1,0:T(8,128)}) fusion(f32[3072]{0:T(1024)S(1)} %reshape.239, bf16[768,3072]{1,0:T(8,128)(2,1)} %all-gather.7.cloned.1.call-done, f32[3,592,768]{2,1,0:T(8,128)} %copy-done, f32[768]{0:T(1024)S(1)} %reshape.238, f32[768]{0:T(1024)S(1)} %reshape.237, ...), kind=kOutput, calls=%fused_computation.8 | convolution fusion | flops 8419774464 | bytes 42942336 | tf_op jit(solution)/shard_map/srd,de->sre/dot_general | solution.py:345
  162.5 13.5 %all-gather.9.cloned.1.call-done = bf16[3072,768]{1,0:T(8,128)(2,1)} async-done(((bf16[192,768]{1,0:T(8,128)(2,1)}), bf16[3072,768]{1,0:T(8,128)(2,1)}) %all-gather.9.cloned.1.call-update) | async-done | bytes 4718608 | tf_op jit(solution)/shard_map/all_gather | solution.py:376
  176.0 14.0 %fusion.51 = (f32[3,592]{1,0:T(4,128)S(1)}, f32[3,592,768]{2,1,0:T(8,128)S(1)}) fusion(f32[768]{0:T(1024)S(1)} %reshape.240, bf16[3,592,3072]{2,1,0:T(8,128)(2,1)} %get-tuple-element.157, bf16[3072,768]{1,0:T(8,128)(2,1)} %all-gather.9.cloned.1.call-done, f32[768]{0:T(1024)S(1)} %reshape.238, f32[768]{0:T(1024)S(1)} %reshape.237, ...), kind=kOutput, calls=%fused_computation.106 | convolution fusion | flops 8389765632 | bytes 26572608 | tf_op jit(solution)/shard_map/srd,de->sre/dot_general | solution.py:345
  190.8 0.8 copy-done.2
  191.7 2.8 fusion.12
  194.5 3.5 convert_reduce_fusion.2
  198.0 20.2 %convert_reduce_fusion = (f32[3072]{0:T(1024)S(1)}, bf16[3,592,3072]{2,1,0:T(8,128)(2,1)}) fusion(f32[3,592,3072]{2,1,0:T(8,128)} %get-tuple-element.158, f32[3072]{0:T(1024)S(1)} %reshape.239, bf16[3,592,768]{2,1,0:T(8,128)(2,1)S(1)} %get-tuple-element.126, bf16[3072,768]{1,0:T(8,128)(2,1)S(1)} %bitcast.107), kind=kOutput, calls=%fused_computation.7 | convolution fusion | flops 8451142656 | bytes 40206336 | tf_op jit(solution)/shard_map/sre,de->srd/dot_general | solution.py:349
  218.2 16.2 %multiply_reduce_fusion = (f32[768]{0:T(1024)S(1)}, f32[3,592]{1,0:T(4,128)S(1)}, f32[3,592]{1,0:T(4,128)S(1)}, f32[768]{0:T(1024)S(1)}, f32[3,592,768]{2,1,0:T(8,128)}) fusion(f32[3,592,768]{2,1,0:T(8,128)S(1)} %bitcast.101, f32[3,592]{1,0:T(4,128)S(1)} %add_rsqrt_fusion.1, f32[3,592]{1,0:T(4,128)S(1)} %broadcast_multiply_fusion.5, f32[768]{0:T(1024)S(1)} %reshape.237, ...), kind=kOutput, calls=%fused_computation.26 | convolution fusion | flops 8411585536 | bytes 34781184 | tf_op jit(solution)/shard_map/sre,de->srd/dot_general | solution.py:349
  234.4 3.9 convert_reduce_fusion.3
  238.3 2.3 bitcast_convert_fusion.2
  240.7 5.1 convolution_convert_fusion.do_ref
  245.8 41.1 %attention_backward.1 = (bf16[3,592,768]{2,1,0:T(8,128)(2,1)}, bf16[3,512,768]{2,1,0:T(8,128)(2,1)}, bf16[3,512,768]{2,1,0:T(8,128)(2,1)}, f32[16,128]{1,0:T(8,128)}) custom-call(s32[3,1,512]{2,1,0:T(1,128)} %broadcast_in_dim.2.perm_ref, bf16[3,592,768]{2,1,0:T(8,128)(2,1)} %get-tuple-element.44.q_ref, bf16[3,512,768]{2,1,0:T(8,128)(2,1)} %get-tuple-element.45.k_ref, ...), custom_call_target="tpu_custom_call" | custom-call | tf_op jit(solution)/shard_map/attention_backward/pallas_call | solution.py:303
  287.0 3.9 fusion.33
  290.9 2.1 fusion.32
  293.0 2.4 bitcast_convert_fusion.5
  295.4 2.4 pad_maximum_fusion
  297.8 6.6 %copy.65 = bf16[768,3072]{1,0:T(8,128)(2,1)} copy(bf16[768,3072]{0,1:T(8,128)(2,1)} %pad_maximum_fusion) | data formatting | bytes 9437184
  304.5 16.2 %bitcast_convert_fusion.1 = bf16[768,3072]{1,0:T(8,128)(2,1)} fusion(bf16[3,592,3072]{2,1,0:T(8,128)(2,1)} %get-tuple-element.163, f32[3,592,768]{2,1,0:T(8,128)} %copy-done, f32[768]{0:T(1024)S(1)} %reshape.238, f32[768]{0:T(1024)S(1)} %reshape.237, f32[3,592]{1,0:T(4,128)S(1)} %add_rsqrt_fusion.1, f32[3,592]{1,0:T(4,128)S(1)} %broadcast_multiply_fusion.5), kind=kOutput, calls=%fused_computation.11 | convolution fusion | flops 8389398528 | bytes 21106560 | tf_op jit(solution)/shard_map/srd,sre->de/dot_general | solution.py:353
  320.9 13.6 %bitcast_convert_fusion = bf16[3072,768]{1,0:T(8,128)(2,1)} fusion(bf16[3,592,3072]{2,1,0:T(8,128)(2,1)} %get-tuple-element.157, bf16[3,592,768]{2,1,0:T(8,128)(2,1)S(1)} %copy-done.8), kind=kOutput, calls=%fused_computation.10 | convolution fusion | flops 8382578688 | bytes 18358272 | tf_op jit(solution)/shard_map/srd,sre->de/dot_general | solution.py:353
  334.5 2.3 convert_reduce_fusion.4
  336.9 2.1 convert_reduce_fusion.5
  339.9 60.8 %all-reduce.4 = bf16[16,600]{1,0:T(8,128)(2,1)S(1)} all-reduce(f32[16,600]{1,0:T(8,128)S(1)} %concatenate.26), channel_id=6, replica_groups=mesh['dp'=2,'fsdp'=16] {'fsdp'}, use_global_device_ids=true, to_apply=%region_23.24.clone | all-reduce | flops 9600 | bytes 57600
  401.3 4.9 psum.31
  406.9 6.4 %fusion.35 = f32[3,512,768]{2,1,0:T(8,128)} fusion(bf16[3,512,768]{2,1,0:T(8,128)(2,1)} %get-tuple-element.51, bf16[768,3072]{1,0:T(8,128)(2,1)} %all-gather.5.cloned.1.call-done), kind=kOutput, calls=%fused_computation.66 | convolution fusion | flops 1811939328 | bytes 8257536 | tf_op jit(solution)/shard_map/sre,de->srd/dot_general | solution.py:349
  413.3 7.9 %convolution_add_fusion = f32[3,592,768]{2,1,0:T(8,128)} fusion(bf16[3,592,768]{2,1,0:T(8,128)(2,1)S(1)} %copy-done.5, f32[3,592]{1,0:T(4,128)S(1)} %broadcast_multiply_fusion, f32[3,592,768]{2,1,0:T(8,128)S(1)} %bitcast.103, f32[3,592]{1,0:T(4,128)S(1)} %broadcast_multiply_fusion.5, f32[3,592]{1,0:T(4,128)S(1)} %broadcast_multiply_fusion.1, ...), kind=kOutput, calls=%fused_computation.59 | convolution fusion | flops 2105966592 | bytes 20306688 | tf_op jit(solution)/shard_map/sre,de->srd/dot_general | solution.py:349
  421.1 2.3 copy.66
  423.4 34.3 %reduce-scatter.6.cloned.1.call-done = bf16[48,3072]{1,0:T(8,128)(2,1)} async-done(((bf16[768,3072]{1,0:T(8,128)(2,1)}), bf16[48,3072]{1,0:T(8,128)(2,1)}) %reduce-scatter.6.cloned.1.call-update) | async-done | bytes 294928 | tf_op jit(solution)/shard_map/reduce_scatter | solution.py:439
  457.7 78.4 %reduce-scatter.8.cloned.1.call-done = bf16[192,768]{1,0:T(8,128)(2,1)} async-done(((bf16[3072,768]{1,0:T(8,128)(2,1)}), bf16[192,768]{1,0:T(8,128)(2,1)}) %reduce-scatter.8.cloned.1.call-update) | async-done | bytes 294928 | tf_op jit(solution)/shard_map/reduce_scatter | solution.py:439
  536.7 3.5 slice.166
  540.2 1.7 slice.167
  542.5 0.9 slice.169
  543.4 7.2 %fusion.16 = f32[3,512,768]{2,1,0:T(8,128)} fusion(f32[3,512,768]{2,1,0:T(8,128)} %fusion.35, f32[3,592,768]{2,1,0:T(8,128)S(1)} %copy-done.3, bf16[3,512,768]{2,1,0:T(8,128)(2,1)S(1)} %copy-done.1, bf16[768,3072]{1,0:T(8,128)(2,1)} %all-gather.5.cloned.1.call-done), kind=kOutput, calls=%fused_computation.42 | convolution fusion | flops 1814298624 | bytes 17694720 | tf_op jit(solution)/shard_map/sre,de->srd/dot_general | solution.py:349
  550.7 34.6 %all-reduce.8.cloned.1.call-done = (bf16[48,3072]{0,1:T(8,128)(2,1)}, bf16[48,3072]{1,0:T(8,128)(2,1)}, bf16[192,768]{1,0:T(8,128)(2,1)}) async-done(((bf16[48,3072]{0,1:T(8,128)(2,1)}, bf16[48,3072]{1,0:T(8,128)(2,1)}, bf16[192,768]{1,0:T(8,128)(2,1)}), (bf16[48,3072]{0,1:T(8,128)(2,1)}, bf16[48,3072]{1,0:T(8,128)(2,1)}, bf16[192,768]{1,0:T(8,128)(2,1)})) %all-reduce.8.cloned.1.call-update) | async-done | bytes 884752 | tf_op jit(solution)/shard_map/psum | solution.py:449
  585.3 1.4 fusion.48
  586.7 0.8 copy.59
  587.5 0.8 copy.60
  589.9 0.9 convert_element_type.204
  590.8 0.9 convert_element_type.206
  (113 shorter events, 11.5 us)
Async XLA Ops:
  7.2 83.9 %all-gather.5.cloned.1.call-start = ((), (), s32[]{:S(2)}) async-start(), calls=%async_computation.3 | async-start | bytes 5013504 | tf_op jit(solution)/shard_map/all_gather | solution.py:376
  9.0 135.9 %all-gather.7.cloned.1.call-start = ((), (), s32[]{:S(2)}) async-start(), calls=%async_computation.4 | async-start | bytes 5013504 | tf_op jit(solution)/shard_map/all_gather | solution.py:376
  9.7 166.3 %all-gather.9.cloned.1.call-start = ((), (), s32[]{:S(2)}) async-start(), calls=%async_computation.5 | async-start | bytes 5013504 | tf_op jit(solution)/shard_map/all_gather | solution.py:376
  10.5 410.7 %reduce-scatter.10.cloned.1.call-start = ((), (), s32[]{:S(2)}) async-start(), calls=%async_computation.8 | async-start | bytes 5013504
  91.1 46.0 %copy-start.9 = (bf16[3,512,768]{2,1,0:T(8,128)(2,1)S(1)}, bf16[3,512,768]{2,1,0:T(8,128)(2,1)}, u32[]{:S(2)}) copy-start(bf16[3,512,768]{2,1,0:T(8,128)(2,1)} %param.23) | copy-start | bytes 7077892
  91.1 46.0 %copy-start.12 = (bf16[3,77,768]{2,1,0:T(8,128)(2,1)S(1)}, bf16[3,77,768]{2,1,0:T(8,128)(2,1)}, u32[]{:S(2)}) copy-start(bf16[3,77,768]{2,1,0:T(8,128)(2,1)} %param.24) | copy-start | bytes 1064452
  141.8 2.3 copy-start
  190.0 1.7 copy-start.2
  190.0 1.7 copy-start.11
  191.7 6.3 %slice-start.4 = ((s8[4718592]{0:T(1024)(128)(4,1)}), s8[4194304]{0:T(1024)(128)(4,1)S(1)}, s32[]{:S(2)}) async-start(s8[4718592]{0:T(1024)(128)(4,1)} %bitcast.106), calls=%async_computation.14 | async-start | bytes 8388608
  194.5 3.5 slice-start.5
  194.5 23.7 %slice-start = ((s8[5455872]{0:T(1024)(128)(4,1)}), s8[4194304]{0:T(1024)(128)(4,1)S(1)}, s32[]{:S(2)}) async-start(s8[5455872]{0:T(1024)(128)(4,1)} %bitcast.100), calls=%async_computation.10 | async-start | bytes 8388608
  197.9 20.2 %copy-start.7 = (bf16[3,592,768]{2,1,0:T(8,128)(2,1)}, bf16[3,592,768]{2,1,0:T(8,128)(2,1)S(1)}, u32[]{:S(2)}) copy-start(bf16[3,592,768]{2,1,0:T(8,128)(2,1)S(1)} %get-tuple-element.126) | copy-start | bytes 8183812
  198.0 20.2 %slice-start.1 = ((s8[5455872]{0:T(1024)(128)(4,1)}), s8[1261568]{0:T(1024)(128)(4,1)S(1)}, s32[]{:S(2)}) async-start(s8[5455872]{0:T(1024)(128)(4,1)} %bitcast.100), calls=%async_computation.11 | async-start | bytes 2523136
  234.4 4.0 copy-start.6
  245.8 41.2 %copy-start.10 = (bf16[3,512,768]{2,1,0:T(8,128)(2,1)S(1)}, bf16[3,512,768]{2,1,0:T(8,128)(2,1)}, u32[]{:S(2)}) copy-start(bf16[3,512,768]{2,1,0:T(8,128)(2,1)} %param.23) | copy-start | bytes 7077892
  287.0 3.9 copy-start.17
  287.0 6.0 copy-start.4
  287.0 6.0 copy-start.13
  304.5 16.4 %copy-start.8 = (bf16[3,592,768]{2,1,0:T(8,128)(2,1)S(1)}, bf16[3,592,768]{2,1,0:T(8,128)(2,1)}, u32[]{:S(2)}) copy-start(bf16[3,592,768]{2,1,0:T(8,128)(2,1)} %copy-done.7) | copy-start | bytes 8183812
  304.5 153.2 %reduce-scatter.6.cloned.1.call-start = ((), (), s32[]{:S(2)}) async-start(), calls=%async_computation.6 | async-start | bytes 5013504 | tf_op jit(solution)/shard_map/reduce_scatter | solution.py:439
  320.8 215.3 %reduce-scatter.8.cloned.1.call-start = ((), (), s32[]{:S(2)}) async-start(), calls=%async_computation.7 | async-start | bytes 5013504 | tf_op jit(solution)/shard_map/reduce_scatter | solution.py:439
  334.4 5.2 copy-start.16
  334.5 250.8 %all-reduce.8.cloned.1.call-start = ((), (), s32[]{:S(2)}) async-start(), calls=%async_computation.9 | async-start | bytes 2752512 | tf_op jit(solution)/shard_map/psum | solution.py:449
  334.5 78.7 %slice-start.2 = ((s8[5455872]{0:T(1024)(128)(4,1)}), s8[1261568]{0:T(1024)(128)(4,1)S(1)}, s32[]{:S(2)}) async-start(s8[5455872]{0:T(1024)(128)(4,1)} %bitcast.102), calls=%async_computation.12 | async-start | bytes 2523136
  406.9 6.4 %slice-start.3 = ((s8[5455872]{0:T(1024)(128)(4,1)}), s8[4194304]{0:T(1024)(128)(4,1)S(1)}, s32[]{:S(2)}) async-start(s8[5455872]{0:T(1024)(128)(4,1)} %bitcast.102), calls=%async_computation.13 | async-start | bytes 8388608
  406.9 6.4 %copy-start.5 = (bf16[3,592,768]{2,1,0:T(8,128)(2,1)S(1)}, bf16[3,592,768]{2,1,0:T(8,128)(2,1)}, u32[]{:S(2)}) copy-start(bf16[3,592,768]{2,1,0:T(8,128)(2,1)} %get-tuple-element.50) | copy-start | bytes 8183812
  421.1 122.3 %copy-start.1 = (bf16[3,512,768]{2,1,0:T(8,128)(2,1)S(1)}, bf16[3,512,768]{2,1,0:T(8,128)(2,1)}, u32[]{:S(2)}) copy-start(bf16[3,512,768]{2,1,0:T(8,128)(2,1)} %get-tuple-element.52) | copy-start | bytes 7077892
  536.1 6.4 %copy-start.3 = (f32[3,592,768]{2,1,0:T(8,128)S(1)}, f32[3,592,768]{2,1,0:T(8,128)}, u32[]{:S(2)}) copy-start(f32[3,592,768]{2,1,0:T(8,128)} %convolution_add_fusion) | copy-start | bytes 16367620
  585.3 4.6 copy-start.15
  585.3 5.5 copy-start.14
Sparse Core Ops, SparseCore 0:
  10.9 56.6 all-gather.4
  69.9 51.9 all-gather.6
  124.2 51.7 all-gather.8
  304.6 74.3 reduce-scatter.9
  383.2 74.4 reduce-scatter.5
  461.4 74.6 reduce-scatter.7
  538.6 46.5 all-reduce.7
